TPU v7x, 32 devices: a whole 2x2x4 slice. The times are simulated.
32 devices in a mesh: gx: 4 (over z), gy: 8 (over y, x, core).
Axes of the slice: x: 2, y: 2, z: 4, core: 2. Of those that a mesh axis runs over, the one named last changes fastest.
Arguments:
- velocity: float32 [2, 2048, 4096], P(None, 'gx', 'gy'), may hold values from -6 to 6
- observed: float32 [2, 2048, 4096], P(None, 'gx', 'gy'), may hold values from -6 to 6
- thickness: float32 [2048, 4096], P('gx', 'gy'), may hold values from 0.5 to 2
- rate_factor: float32 [2048, 4096], P('gx', 'gy'), may hold values from 0.5 to 2
- friction: float32 [2048, 4096], P('gx', 'gy'), may hold values from 0.1 to 10
- cell_mask: int32 [2048, 4096], P('gx', 'gy'), may hold values from 0 to 2
- front_codes: int32 [2048, 4096], P('gx', 'gy'), may hold values from 0 to 15
- modes_x: bfloat16 [2048, 512], P('gx'), may hold values from -0.125 to 0.125
- modes_y: bfloat16 [4096, 512], P('gy'), may hold values from -0.09375 to 0.09375
Outputs:
- adjoint: float32 [2, 2048, 4096], P(None, 'gx', 'gy')
- coefficients: float32 [512, 512], P('gx', 'gy')
Inputs may be any that keep to these rules, and one draw needn't show every extreme that they name: `cell_mask`: 0 is ocean, 1 floating ice, 2 grounded ice. `front_codes`: bit 0, 1, 2, 3 marks a calving front on the cell's lower first-dimension, upper first-dimension, lower second-dimension, upper second-dimension face.
All inputs are finite; a program needn't handle non-finite values.
Results may differ from a plain program's by a relative error of at most 0.0029.
Values sent between devices are 32-bit elements; how exact they have to be, the bound alone decides.
A program may use at most 128 MiB of HBM per device.

v0:
```python
import jax
import jax.numpy as jnp
from jax import lax
from jax.sharding import PartitionSpec as P

SWEEPS = 3


def padded_2(array, sides, width):
    for axis, dim in sides:
        count, length = (lax.axis_size(axis), array.shape[dim])
        up = [(i, (i + 1) % count) for i in range(count - 1)]
        down = [(j, i) for i, j in up]
        last = lax.slice_in_dim(array, length - width, length, axis=dim)
        leading = lax.slice_in_dim(array, 0, width, axis=dim)
        before = lax.ppermute(last, axis, up)
        after = lax.ppermute(leading, axis, down)
        array = jnp.concatenate([before, array, after], axis=dim)
    return array


def viscosity(padded, stiffness):
    along_x = (padded[:, 2:, 1:-1] - padded[:, :-2, 1:-1]) * 0.5
    along_y = (padded[:, 1:-1, 2:] - padded[:, 1:-1, :-2]) * 0.5
    shear = along_y[0] + along_x[1]
    strain = (
        along_x[0] * along_x[0]
        + along_y[1] * along_y[1]
        + along_x[0] * along_y[1]
        + 0.25 * shear * shear
    )
    return stiffness * 0.5 * (strain + 0.01) ** (-1.0 / 3.0)


def face_terms(eta_pad):
    center = eta_pad[1:-1, 1:-1]
    lower_x = jnp.sqrt(center * eta_pad[:-2, 1:-1])
    upper_x = jnp.sqrt(center * eta_pad[2:, 1:-1])
    lower_y = jnp.sqrt(center * eta_pad[1:-1, :-2])
    upper_y = jnp.sqrt(center * eta_pad[1:-1, 2:])
    return (lower_x, upper_x, lower_y, upper_y)


def front_count(front_codes):
    total = jnp.zeros(front_codes.shape, jnp.float32)
    for bit_index in range(4):
        total = total + (jnp.right_shift(front_codes, bit_index) & 1).astype(jnp.float32)
    return total


def relax(adjoint_pad, faces, rhs, diagonal_sum):
    lower_x, upper_x, lower_y, upper_y = faces
    x_weights = jnp.array([4.0, 1.0], jnp.float32).reshape(2, 1, 1)
    y_weights = jnp.array([1.0, 4.0], jnp.float32).reshape(2, 1, 1)
    near_x = lower_x * adjoint_pad[:, :-2, 1:-1] + upper_x * adjoint_pad[:, 2:, 1:-1]
    near_y = lower_y * adjoint_pad[:, 1:-1, :-2] + upper_y * adjoint_pad[:, 1:-1, 2:]
    return (rhs + x_weights * near_x + y_weights * near_y) / diagonal_sum


def shards(
    velocity, observed, thickness, rate_factor, friction, cell_mask, front_codes, modes_x, modes_y
):
    ice = (cell_mask >= 1).astype(jnp.float32)
    grounded = (cell_mask == 2).astype(jnp.float32)
    stiffness = thickness * ice * rate_factor
    x_weights = jnp.array([4.0, 1.0], jnp.float32).reshape(2, 1, 1)
    y_weights = jnp.array([1.0, 4.0], jnp.float32).reshape(2, 1, 1)
    sweeps_total = SWEEPS
    vel_pad = padded_2(velocity, (("gx", 1), ("gy", 2)), 1)
    eta = viscosity(vel_pad, stiffness)
    eta_pad = padded_2(eta, (("gx", 0), ("gy", 1)), 1)
    faces = face_terms(eta_pad)
    lower_x, upper_x, lower_y, upper_y = faces
    extra = 2.0 * eta * front_count(front_codes) + friction * grounded + 1.0
    diagonal_sum = x_weights * (lower_x + upper_x) + y_weights * (lower_y + upper_y) + extra
    rhs = ice * (velocity - observed)
    adjoint = rhs / diagonal_sum
    for sweep in range(sweeps_total - 1):
        adjoint_pad = padded_2(adjoint, (("gx", 1), ("gy", 2)), 1)
        adjoint = relax(adjoint_pad, faces, rhs, diagonal_sum)
    gradient = (
        -(friction * grounded) * (velocity[0] * adjoint[0] + velocity[1] * adjoint[1])
    ).astype(jnp.bfloat16)
    table = modes_x
    row_share = lax.psum_scatter(
        lax.dot_general(
            table, gradient, (((0,), (0,)), ((), ())), preferred_element_type=jnp.float32
        ),
        "gx",
        scatter_dimension=0,
        tiled=True,
    )
    table = modes_y.astype(jnp.float32)
    flipped = lax.psum_scatter(
        lax.dot_general(
            table, row_share, (((0,), (1,)), ((), ())), precision=lax.Precision.HIGHEST
        ),
        "gy",
        scatter_dimension=0,
        tiled=True,
    )
    coefficients = flipped.T
    return (adjoint, coefficients)


def solution(mesh):
    placed = (
        P(None, "gx", "gy"),
        P(None, "gx", "gy"),
        P("gx", "gy"),
        P("gx", "gy"),
        P("gx", "gy"),
        P("gx", "gy"),
        P("gx", "gy"),
        P("gx", None),
        P("gy", None),
    )
    return jax.shard_map(
        shards,
        mesh=mesh,
        in_specs=placed,
        out_specs=(P(None, "gx", "gy"), P("gx", "gy")),
        check_vma=False,
    )
```

profile of v0, /device:TPU:0, one launch (start us, length us, event | category | flops | bytes accessed | tf_op | source)
XLA Modules:
  0.0 191.6 jit_solution(13860215947696083670)
XLA Ops:
  9.4 5.7 %collective-permute-start.1 = (f32[2,1,512]{2,1,0:T(1,128)S(1)}, f32[2,1,512]{2,1,0:T(1,128)S(1)}, u32[]{:S(2)}, u32[]{:S(2)}) collective-permute-start(f32[2,1,512]{2,1,0:T(1,128)S(1)} %get-tuple-element.32), channel_id=1, source_target_pairs={{0,8},{8,16},{16,24},{1,9},{9,17},{17,25},{2,10},{10,18},{18,26},{... | collective-permute-start | bytes 12296 | tf_op jit(solution)/shard_map/ppermute | solution.py:16
  15.1 1.3 collective-permute-done.1
  16.4 2.2 %pad_maximum_fusion.40 = (f32[2,514,1]{2,1,0:T(8,128)}, f32[2,514,1]{2,1,0:T(8,128)S(1)}) fusion(f32[2,1,512]{2,1,0:T(1,128)S(1)} %collective-permute-done, f32[2,512,512]{2,1,0:T(8,128)} %param.15, f32[2,1,512]{2,1,0:T(1,128)S(1)} %collective-permute-done.1), kind=kLoop, calls=%fused_computation.94 | loop fusion | flops 4112 | bytes 2113568 | tf_op jit(solution)/shard_map/slice | solution.py:15
  19.8 1.3 collective-permute-start.2
  21.3 3.0 %collective-permute-start.3 = (f32[2,514,1]{1,0,2:T(2,128)S(1)}, f32[2,514,1]{1,0,2:T(2,128)S(1)}, u32[]{:S(2)}, u32[]{:S(2)}) collective-permute-start(f32[2,514,1]{1,0,2:T(2,128)S(1)} %copy.53), channel_id=1, source_target_pairs={{0,1},{1,2},{2,3},{3,4},{4,5},{5,6},{6,7},{8,9},{9,10},{10,11},{11... | collective-permute-start | bytes 12344 | tf_op jit(solution)/shard_map/ppermute | solution.py:16
  26.3 3.6 %fusion.23 = (f32[2,512,512]{2,1,0:T(8,128)S(1)}, f32[2,512,512]{2,1,0:T(8,128)S(1)}) fusion(f32[2,514,1]{2,1,0:T(8,128)} %copy.54, f32[2,1,512]{2,1,0:T(1,128)S(1)} %collective-permute-done, f32[2,512,512]{2,1,0:T(8,128)S(1)} %copy-done.1, f32[2,1,512]{2,1,0:T(1,128)S(1)} %collective-permute-done.1, f32[2,514,1]{2,1,0:T(8,128)S(1)} %copy.52), kind=kLoop, calls=%fused_computation.40 | loop fusion | flops 6291456 | bytes 6307872 | tf_op jit(solution)/shard_map/mul | solution.py:24
  29.9 2.4 %add_add_fusion.1 = (f32[512,512]{1,0:T(8,128)S(1)}, f32[512,512]{1,0:T(8,128)S(1)}, pred[512,512]{1,0:T(8,128)(4,1)S(1)}) fusion(s32[512,512]{1,0:T(8,128)S(1)} %copy-done.13, f32[512,512]{1,0:T(8,128)S(1)} %copy-done.8, s32[512,512]{1,0:T(8,128)S(1)} %copy-done.10, f32[2,512,512]{2,1,0:T(8,128)S(1)} %get-tuple-element.24, ...), kind=kLoop, calls=%fused_computation.84 | loop fusion | flops 9437184 | bytes 11796480 | tf_op jit(solution)/shard_map/add | solution.py:74
  32.3 4.2 %collective-permute-start.4 = (f32[1,512]{1,0:T(1,128)S(1)}, f32[1,512]{1,0:T(1,128)S(1)}, u32[]{:S(2)}, u32[]{:S(2)}) collective-permute-start(f32[1,512]{1,0:T(1,128)S(1)} %get-tuple-element.38), channel_id=1, source_target_pairs={{0,8},{8,16},{16,24},{1,9},{9,17},{17,25},{2,10},{10,18},{18,26},{... | collective-permute-start | bytes 6152 | tf_op jit(solution)/shard_map/ppermute | solution.py:16
  36.5 1.3 collective-permute-start.5
  37.8 4.2 %collective-permute-done.5 = f32[1,512]{1,0:T(1,128)S(1)} collective-permute-done((f32[1,512]{1,0:T(1,128)S(1)}, f32[1,512]{1,0:T(1,128)S(1)}, u32[]{:S(2)}, u32[]{:S(2)}) %collective-permute-start.5) | collective-permute-done | bytes 2080 | tf_op jit(solution)/shard_map/ppermute | solution.py:17
  42.1 2.0 %collective-permute-start.6 = (f32[514,1]{1,0:T(8,128)S(1)}, f32[514,1]{1,0:T(8,128)S(1)}, u32[]{:S(2)}, u32[]{:S(2)}) collective-permute-start(f32[514,1]{1,0:T(8,128)S(1)} %get-tuple-element.36), channel_id=1, source_target_pairs={{0,1},{1,2},{2,3},{3,4},{4,5},{5,6},{6,7},{8,9},{9,10},{10,11},{11... | collective-permute-start | bytes 6176 | tf_op jit(solution)/shard_map/ppermute | solution.py:16
  45.7 5.1 %collective-permute-done.7 = f32[514,1]{1,0:T(8,128)S(1)} collective-permute-done((f32[514,1]{1,0:T(8,128)S(1)}, f32[514,1]{1,0:T(8,128)S(1)}, u32[]{:S(2)}, u32[]{:S(2)}) %collective-permute-start.7) | collective-permute-done | bytes 2088 | tf_op jit(solution)/shard_map/ppermute | solution.py:17
  50.8 3.5 %fusion.47 = (f32[512,512]{1,0:T(8,128)S(1)}, f32[512,512]{1,0:T(8,128)}, f32[512,512]{1,0:T(8,128)}, f32[512,512]{1,0:T(8,128)S(1)}, f32[512,512]{1,0:T(8,128)}, /*index=5*/f32[512,512]{1,0:T(8,128)}) fusion(f32[512,512]{1,0:T(8,128)S(1)} %get-tuple-element.17, f32[1,512]{1,0:T(1,128)S(1)} %collective-permute-done.5, ...), kind=kLoop, calls=%fused_computation.101 | loop fusion | flops 3670016 | bytes 7348240 | tf_op jit(solution)/shard_map/add | solution.py:75
  54.3 2.5 %fusion.26 = (f32[2,512,512]{2,1,0:T(8,128)S(1)}, f32[2,512,512]{2,1,0:T(8,128)}) fusion(f32[512,512]{1,0:T(8,128)S(1)} %get-tuple-element.16, f32[512,512]{1,0:T(8,128)S(1)} %get-tuple-element.33, f32[2]{0:T(128)S(1)} %copy-done.17, f32[512,512]{1,0:T(8,128)S(1)} %get-tuple-element.10, f32[2]{0:T(128)S(1)} %copy-done.18, f32[2,512,512]{2,1,0:T(8,128)S(1)} %copy-done.1, ...), kind=kLoop, calls=%fused_computation.51 | loop fusion | flops 3670016 | bytes 12582928 | tf_op jit(solution)/shard_map/div | solution.py:77
  56.8 3.5 %collective-permute-start.8 = (f32[2,1,512]{2,1,0:T(1,128)S(1)}, f32[2,1,512]{2,1,0:T(1,128)S(1)}, u32[]{:S(2)}, u32[]{:S(2)}) collective-permute-start(f32[2,1,512]{2,1,0:T(1,128)S(1)} %get-tuple-element.29), channel_id=1, source_target_pairs={{0,8},{8,16},{16,24},{1,9},{9,17},{17,25},{2,10},{10,18},{18,26},{... | collective-permute-start | bytes 12296 | tf_op jit(solution)/shard_map/ppermute | solution.py:16
  60.3 1.3 collective-permute-start.9
  61.6 4.2 %collective-permute-done.9 = f32[2,1,512]{2,1,0:T(1,128)S(1)} collective-permute-done((f32[2,1,512]{2,1,0:T(1,128)S(1)}, f32[2,1,512]{2,1,0:T(1,128)S(1)}, u32[]{:S(2)}, u32[]{:S(2)}) %collective-permute-start.9) | collective-permute-done | bytes 4128 | tf_op jit(solution)/shard_map/ppermute | solution.py:17
  68.1 6.3 %collective-permute-start.10 = (f32[2,514,1]{1,0,2:T(2,128)S(1)}, f32[2,514,1]{1,0,2:T(2,128)S(1)}, u32[]{:S(2)}, u32[]{:S(2)}) collective-permute-start(f32[2,514,1]{1,0,2:T(2,128)S(1)} %copy.55), channel_id=1, source_target_pairs={{0,1},{1,2},{2,3},{3,4},{4,5},{5,6},{6,7},{8,9},{9,10},{10,11},{11... | collective-permute-start | bytes 12344 | tf_op jit(solution)/shard_map/ppermute | solution.py:16
  74.6 1.3 collective-permute-start.11
  76.1 2.3 %collective-permute-done.11 = f32[2,514,1]{1,0,2:T(2,128)S(1)} collective-permute-done((f32[2,514,1]{1,0,2:T(2,128)S(1)}, f32[2,514,1]{1,0,2:T(2,128)S(1)}, u32[]{:S(2)}, u32[]{:S(2)}) %collective-permute-start.11) | collective-permute-done | bytes 4144 | tf_op jit(solution)/shard_map/ppermute | solution.py:17
  79.5 8.5 %fusion.15 = f32[2,512,512]{2,1,0:T(8,128)S(1)} fusion(f32[2,514,1]{2,1,0:T(8,128)} %copy.58, f32[2,1,512]{2,1,0:T(1,128)S(1)} %collective-permute-done.9, f32[2,512,512]{2,1,0:T(8,128)} %copy-done.2, f32[2,1,512]{2,1,0:T(1,128)S(1)} %collective-permute-done.8, f32[2,514,1]{2,1,0:T(8,128)S(1)} %copy.56, f32[2,512,512]{2,1,0:T(8,128)} %get-tuple-element.9, ...), kind=kLoop, calls=%fused_computation.24 | loop fusion | flops 12058624 | bytes 13647920 | tf_op jit(solution)/shard_map/div | solution.py:57
  88.0 3.5 %collective-permute-start.12 = (f32[2,1,512]{2,1,0:T(1,128)S(1)}, f32[2,1,512]{2,1,0:T(1,128)S(1)}, u32[]{:S(2)}, u32[]{:S(2)}) collective-permute-start(f32[2,1,512]{2,1,0:T(1,128)S(1)} %get-tuple-element.27), channel_id=1, source_target_pairs={{0,8},{8,16},{16,24},{1,9},{9,17},{17,25},{2,10},{10,18},{18,26},{... | collective-permute-start | bytes 12296 | tf_op jit(solution)/shard_map/ppermute | solution.py:16
  92.8 4.2 %collective-permute-done.13 = f32[2,1,512]{2,1,0:T(1,128)S(1)} collective-permute-done((f32[2,1,512]{2,1,0:T(1,128)S(1)}, f32[2,1,512]{2,1,0:T(1,128)S(1)}, u32[]{:S(2)}, u32[]{:S(2)}) %collective-permute-start.13) | collective-permute-done | bytes 4128 | tf_op jit(solution)/shard_map/ppermute | solution.py:17
  99.3 2.8 %collective-permute-start.14 = (f32[2,514,1]{1,0,2:T(2,128)S(1)}, f32[2,514,1]{1,0,2:T(2,128)S(1)}, u32[]{:S(2)}, u32[]{:S(2)}) collective-permute-start(f32[2,514,1]{1,0,2:T(2,128)S(1)} %copy.59), channel_id=1, source_target_pairs={{0,1},{1,2},{2,3},{3,4},{4,5},{5,6},{6,7},{8,9},{9,10},{10,11},{11... | collective-permute-start | bytes 12344 | tf_op jit(solution)/shard_map/ppermute | solution.py:16
  102.4 1.5 collective-permute-start.15
  104.1 2.3 %collective-permute-done.15 = f32[2,514,1]{1,0,2:T(2,128)S(1)} collective-permute-done((f32[2,514,1]{1,0,2:T(2,128)S(1)}, f32[2,514,1]{1,0,2:T(2,128)S(1)}, u32[]{:S(2)}, u32[]{:S(2)}) %collective-permute-start.15) | collective-permute-done | bytes 4144 | tf_op jit(solution)/shard_map/ppermute | solution.py:17
  107.5 8.5 %fusion.4 = f32[2,512,512]{2,1,0:T(8,128)S(1)} fusion(f32[2,514,1]{2,1,0:T(8,128)} %copy.62, f32[2,1,512]{2,1,0:T(1,128)S(1)} %collective-permute-done.13, f32[2,512,512]{2,1,0:T(8,128)} %copy-done.3, f32[2,1,512]{2,1,0:T(1,128)S(1)} %collective-permute-done.12, f32[2,514,1]{2,1,0:T(8,128)S(1)} %copy.60, f32[2,512,512]{2,1,0:T(8,128)} %get-tuple-element.9, ...), kind=kLoop, calls=%fused_computation.5 | loop fusion | flops 12058624 | bytes 13647920 | tf_op jit(solution)/shard_map/div | solution.py:57
  116.0 1.3 copy-done.7
  117.3 2.0 %convolution_bitcast_fusion = f32[512,512]{0,1:T(8,128)} fusion(bf16[512,512]{1,0:T(8,128)(2,1)S(1)} %copy-done, f32[2,512,512]{2,1,0:T(8,128)S(1)} %fusion.4, f32[2,512,512]{2,1,0:T(8,128)S(1)} %copy-done.1, f32[512,512]{1,0:T(8,128)S(1)} %copy-done.9, s32[512,512]{1,0:T(8,128)S(1)} %copy-done.11), kind=kOutput, calls=%fused_computation.54 | convolution fusion | flops 270532608 | bytes 7864320 | tf_op jit(solution)/shard_map/dot_general | solution.py:86
  119.4 29.1 %reduce-scatter.5.cloned.1.call-done = f32[128,512]{0,1:T(8,128)} async-done(((f32[512,512]{0,1:T(8,128)}), f32[128,512]{0,1:T(8,128)}) %reduce-scatter.5.cloned.1.call-update) | async-done | bytes 262160 | tf_op jit(solution)/shard_map/reduce_scatter | solution.py:85
  148.6 1.4 convolution_bitcast_fusion.1
  150.8 33.9 %reduce-scatter.7.cloned.1.call-done = f32[64,128]{1,0:T(8,128)} async-done(((f32[512,128]{1,0:T(8,128)}), f32[64,128]{1,0:T(8,128)}) %reduce-scatter.7.cloned.1.call-update) | async-done | bytes 32784
  (74 shorter events, 17.0 us)
Async XLA Ops:
  7.2 110.1 %copy-start = (bf16[512,512]{1,0:T(8,128)(2,1)S(1)}, bf16[512,512]{1,0:T(8,128)(2,1)}, u32[]{:S(2)}) copy-start(bf16[512,512]{1,0:T(8,128)(2,1)} %param.22) | copy-start | bytes 1572868
  7.2 141.4 %reduce-scatter.5.cloned.1.call-start = ((), (), s32[]{:S(2)}) async-start(), calls=%async_computation.2 | async-start | bytes 1310720 | tf_op jit(solution)/shard_map/reduce_scatter | solution.py:85
  8.1 7.0 %collective-permute-start = (f32[2,1,512]{2,1,0:T(1,128)S(1)}, f32[2,1,512]{2,1,0:T(1,128)S(1)}, u32[]{:S(2)}, u32[]{:S(2)}) collective-permute-start(f32[2,1,512]{2,1,0:T(1,128)S(1)} %get-tuple-element.31), channel_id=1, source_target_pairs={{8,0},{16,8},{24,16},{9,1},{17,9},{25,17},{10,2},{18,10},{26,18},{... | collective-permute-start | bytes 12296 | tf_op jit(solution)/shard_map/ppermute | solution.py:17
  9.3 16.9 %copy-start.1 = (f32[2,512,512]{2,1,0:T(8,128)S(1)}, f32[2,512,512]{2,1,0:T(8,128)}, u32[]{:S(2)}) copy-start(f32[2,512,512]{2,1,0:T(8,128)} %param.15) | copy-start | bytes 6291460
  9.4 7.0 %collective-permute-start.1 = (f32[2,1,512]{2,1,0:T(1,128)S(1)}, f32[2,1,512]{2,1,0:T(1,128)S(1)}, u32[]{:S(2)}, u32[]{:S(2)}) collective-permute-start(f32[2,1,512]{2,1,0:T(1,128)S(1)} %get-tuple-element.32), channel_id=1, source_target_pairs={{0,8},{8,16},{16,24},{1,9},{9,17},{17,25},{2,10},{10,18},{18,26},{... | collective-permute-start | bytes 12296 | tf_op jit(solution)/shard_map/ppermute | solution.py:16
  19.8 4.6 %collective-permute-start.2 = (f32[2,514,1]{1,0,2:T(2,128)S(1)}, f32[2,514,1]{1,0,2:T(2,128)S(1)}, u32[]{:S(2)}, u32[]{:S(2)}) collective-permute-start(f32[2,514,1]{1,0,2:T(2,128)S(1)} %copy.51), channel_id=1, source_target_pairs={{1,0},{2,1},{3,2},{4,3},{5,4},{6,5},{7,6},{9,8},{10,9},{11,10},{12... | collective-permute-start | bytes 12344 | tf_op jit(solution)/shard_map/ppermute | solution.py:17
  21.3 3.8 %collective-permute-start.3 = (f32[2,514,1]{1,0,2:T(2,128)S(1)}, f32[2,514,1]{1,0,2:T(2,128)S(1)}, u32[]{:S(2)}, u32[]{:S(2)}) collective-permute-start(f32[2,514,1]{1,0,2:T(2,128)S(1)} %copy.53), channel_id=1, source_target_pairs={{0,1},{1,2},{2,3},{3,4},{4,5},{5,6},{6,7},{8,9},{9,10},{10,11},{11... | collective-permute-start | bytes 12344 | tf_op jit(solution)/shard_map/ppermute | solution.py:16
  26.2 3.7 %copy-start.13 = (s32[512,512]{1,0:T(8,128)S(1)}, s32[512,512]{1,0:T(8,128)}, u32[]{:S(2)}) copy-start(s32[512,512]{1,0:T(8,128)} %param.21) | copy-start | bytes 3145732
  26.2 3.7 %copy-start.14 = (f32[512,512]{1,0:T(8,128)S(1)}, f32[512,512]{1,0:T(8,128)}, u32[]{:S(2)}) copy-start(f32[512,512]{1,0:T(8,128)} %param.18) | copy-start | bytes 3145732
  26.2 3.7 %copy-start.15 = (f32[512,512]{1,0:T(8,128)S(1)}, f32[512,512]{1,0:T(8,128)}, u32[]{:S(2)}) copy-start(f32[512,512]{1,0:T(8,128)} %param.17) | copy-start | bytes 3145732
  32.3 21.9 %copy-start.4 = (f32[512,512]{1,0:T(8,128)}, f32[512,512]{1,0:T(8,128)S(1)}, u32[]{:S(2)}) copy-start(f32[512,512]{1,0:T(8,128)S(1)} %get-tuple-element.16) | copy-start | bytes 3145732
  32.3 5.5 %collective-permute-start.4 = (f32[1,512]{1,0:T(1,128)S(1)}, f32[1,512]{1,0:T(1,128)S(1)}, u32[]{:S(2)}, u32[]{:S(2)}) collective-permute-start(f32[1,512]{1,0:T(1,128)S(1)} %get-tuple-element.38), channel_id=1, source_target_pairs={{0,8},{8,16},{16,24},{1,9},{9,17},{17,25},{2,10},{10,18},{18,26},{... | collective-permute-start | bytes 6152 | tf_op jit(solution)/shard_map/ppermute | solution.py:16
  36.5 5.5 %collective-permute-start.5 = (f32[1,512]{1,0:T(1,128)S(1)}, f32[1,512]{1,0:T(1,128)S(1)}, u32[]{:S(2)}, u32[]{:S(2)}) collective-permute-start(f32[1,512]{1,0:T(1,128)S(1)} %get-tuple-element.39), channel_id=1, source_target_pairs={{8,0},{16,8},{24,16},{9,1},{17,9},{25,17},{10,2},{18,10},{26,18},{... | collective-permute-start | bytes 6152 | tf_op jit(solution)/shard_map/ppermute | solution.py:17
  42.1 3.5 %collective-permute-start.6 = (f32[514,1]{1,0:T(8,128)S(1)}, f32[514,1]{1,0:T(8,128)S(1)}, u32[]{:S(2)}, u32[]{:S(2)}) collective-permute-start(f32[514,1]{1,0:T(8,128)S(1)} %get-tuple-element.36), channel_id=1, source_target_pairs={{0,1},{1,2},{2,3},{3,4},{4,5},{5,6},{6,7},{8,9},{9,10},{10,11},{11... | collective-permute-start | bytes 6176 | tf_op jit(solution)/shard_map/ppermute | solution.py:16
  44.2 6.6 %collective-permute-start.7 = (f32[514,1]{1,0:T(8,128)S(1)}, f32[514,1]{1,0:T(8,128)S(1)}, u32[]{:S(2)}, u32[]{:S(2)}) collective-permute-start(f32[514,1]{1,0:T(8,128)S(1)} %get-tuple-element.37), channel_id=1, source_target_pairs={{1,0},{2,1},{3,2},{4,3},{5,4},{6,5},{7,6},{9,8},{10,9},{11,10},{12... | collective-permute-start | bytes 6176 | tf_op jit(solution)/shard_map/ppermute | solution.py:17
  45.6 8.6 %copy-start.12 = (f32[2,512,512]{2,1,0:T(8,128)S(1)}, f32[2,512,512]{2,1,0:T(8,128)}, u32[]{:S(2)}) copy-start(f32[2,512,512]{2,1,0:T(8,128)} %param.16) | copy-start | bytes 6291460
  45.6 8.6 %copy-start.17 = (f32[2]{0:T(128)S(1)}, f32[2]{0:T(128)}, u32[]{:S(2)}) copy-start(f32[2]{0:T(128)} %constant.29.clone) | copy-start | bytes 28
  45.6 8.6 %copy-start.18 = (f32[2]{0:T(128)S(1)}, f32[2]{0:T(128)}, u32[]{:S(2)}) copy-start(f32[2]{0:T(128)} %constant.28.clone) | copy-start | bytes 28
  56.8 9.0 %copy-start.2 = (f32[2,512,512]{2,1,0:T(8,128)}, f32[2,512,512]{2,1,0:T(8,128)S(1)}, u32[]{:S(2)}) copy-start(f32[2,512,512]{2,1,0:T(8,128)S(1)} %get-tuple-element.8) | copy-start | bytes 6291460
  56.8 4.8 %collective-permute-start.8 = (f32[2,1,512]{2,1,0:T(1,128)S(1)}, f32[2,1,512]{2,1,0:T(1,128)S(1)}, u32[]{:S(2)}, u32[]{:S(2)}) collective-permute-start(f32[2,1,512]{2,1,0:T(1,128)S(1)} %get-tuple-element.29), channel_id=1, source_target_pairs={{0,8},{8,16},{16,24},{1,9},{9,17},{17,25},{2,10},{10,18},{18,26},{... | collective-permute-start | bytes 12296 | tf_op jit(solution)/shard_map/ppermute | solution.py:16
  60.3 5.5 %collective-permute-start.9 = (f32[2,1,512]{2,1,0:T(1,128)S(1)}, f32[2,1,512]{2,1,0:T(1,128)S(1)}, u32[]{:S(2)}, u32[]{:S(2)}) collective-permute-start(f32[2,1,512]{2,1,0:T(1,128)S(1)} %get-tuple-element.30), channel_id=1, source_target_pairs={{8,0},{16,8},{24,16},{9,1},{17,9},{25,17},{10,2},{18,10},{26,18},{... | collective-permute-start | bytes 12296 | tf_op jit(solution)/shard_map/ppermute | solution.py:17
  68.1 7.8 %collective-permute-start.10 = (f32[2,514,1]{1,0,2:T(2,128)S(1)}, f32[2,514,1]{1,0,2:T(2,128)S(1)}, u32[]{:S(2)}, u32[]{:S(2)}) collective-permute-start(f32[2,514,1]{1,0,2:T(2,128)S(1)} %copy.55), channel_id=1, source_target_pairs={{0,1},{1,2},{2,3},{3,4},{4,5},{5,6},{6,7},{8,9},{9,10},{10,11},{11... | collective-permute-start | bytes 12344 | tf_op jit(solution)/shard_map/ppermute | solution.py:16
  74.6 3.8 %collective-permute-start.11 = (f32[2,514,1]{1,0,2:T(2,128)S(1)}, f32[2,514,1]{1,0,2:T(2,128)S(1)}, u32[]{:S(2)}, u32[]{:S(2)}) collective-permute-start(f32[2,514,1]{1,0,2:T(2,128)S(1)} %copy.57), channel_id=1, source_target_pairs={{1,0},{2,1},{3,2},{4,3},{5,4},{6,5},{7,6},{9,8},{10,9},{11,10},{12... | collective-permute-start | bytes 12344 | tf_op jit(solution)/shard_map/ppermute | solution.py:17
  88.0 9.0 %copy-start.3 = (f32[2,512,512]{2,1,0:T(8,128)}, f32[2,512,512]{2,1,0:T(8,128)S(1)}, u32[]{:S(2)}) copy-start(f32[2,512,512]{2,1,0:T(8,128)S(1)} %fusion.15) | copy-start | bytes 6291460
  88.0 4.8 %collective-permute-start.12 = (f32[2,1,512]{2,1,0:T(1,128)S(1)}, f32[2,1,512]{2,1,0:T(1,128)S(1)}, u32[]{:S(2)}, u32[]{:S(2)}) collective-permute-start(f32[2,1,512]{2,1,0:T(1,128)S(1)} %get-tuple-element.27), channel_id=1, source_target_pairs={{0,8},{8,16},{16,24},{1,9},{9,17},{17,25},{2,10},{10,18},{18,26},{... | collective-permute-start | bytes 12296 | tf_op jit(solution)/shard_map/ppermute | solution.py:16
  91.5 5.5 %collective-permute-start.13 = (f32[2,1,512]{2,1,0:T(1,128)S(1)}, f32[2,1,512]{2,1,0:T(1,128)S(1)}, u32[]{:S(2)}, u32[]{:S(2)}) collective-permute-start(f32[2,1,512]{2,1,0:T(1,128)S(1)} %get-tuple-element.28), channel_id=1, source_target_pairs={{8,0},{16,8},{24,16},{9,1},{17,9},{25,17},{10,2},{18,10},{26,18},{... | collective-permute-start | bytes 12296 | tf_op jit(solution)/shard_map/ppermute | solution.py:17
  99.3 4.6 %collective-permute-start.14 = (f32[2,514,1]{1,0,2:T(2,128)S(1)}, f32[2,514,1]{1,0,2:T(2,128)S(1)}, u32[]{:S(2)}, u32[]{:S(2)}) collective-permute-start(f32[2,514,1]{1,0,2:T(2,128)S(1)} %copy.59), channel_id=1, source_target_pairs={{0,1},{1,2},{2,3},{3,4},{4,5},{5,6},{6,7},{8,9},{9,10},{10,11},{11... | collective-permute-start | bytes 12344 | tf_op jit(solution)/shard_map/ppermute | solution.py:16
  102.4 4.0 %collective-permute-start.15 = (f32[2,514,1]{1,0,2:T(2,128)S(1)}, f32[2,514,1]{1,0,2:T(2,128)S(1)}, u32[]{:S(2)}, u32[]{:S(2)}) collective-permute-start(f32[2,514,1]{1,0,2:T(2,128)S(1)} %copy.61), channel_id=1, source_target_pairs={{1,0},{2,1},{3,2},{4,3},{5,4},{6,5},{7,6},{9,8},{10,9},{11,10},{12... | collective-permute-start | bytes 12344 | tf_op jit(solution)/shard_map/ppermute | solution.py:17
  107.5 9.8 %copy-start.9 = (f32[512,512]{1,0:T(8,128)S(1)}, f32[512,512]{1,0:T(8,128)}, u32[]{:S(2)}) copy-start(f32[512,512]{1,0:T(8,128)} %param.19) | copy-start | bytes 3145732
  107.5 9.8 %copy-start.11 = (s32[512,512]{1,0:T(8,128)S(1)}, s32[512,512]{1,0:T(8,128)}, u32[]{:S(2)}) copy-start(s32[512,512]{1,0:T(8,128)} %param.20) | copy-start | bytes 3145732
  117.3 31.2 %copy-start.16 = (bf16[512,512]{1,0:T(8,128)(2,1)S(1)}, bf16[512,512]{1,0:T(8,128)(2,1)}, u32[]{:S(2)}) copy-start(bf16[512,512]{1,0:T(8,128)(2,1)} %param.23) | copy-start | bytes 1572868
  119.4 65.4 %reduce-scatter.7.cloned.1.call-start = ((), (), s32[]{:S(2)}) async-start(), calls=%async_computation.3 | async-start | bytes 294912
  (5 other events, 13.7 us)
Sparse Core Ops, SparseCore 0:
  119.5 29.0 reduce-scatter.4
  152.4 32.2 reduce-scatter.6
where the time goes:
time: 192 us
  waiting for transfers between devices  87.2 us (45%)
  starting transfers between devices  41.6 us (22%)
  other arithmetic  33.4 us (17%)
  between operations  14.5 us (8%)
  local copies, waits for them, and re-layouts  11.4 us (6%)
  matrix products  3.42 us (2%)
    unnamed x3, waiting for transfers between devices  33.9 us
    ppermute x8, starting transfers between devices, padded_2(): before = lax.ppermute(last, axis, up)  31 us
    reduce_scatter x1, waiting for transfers between devices, shards(): lax.psum_scatter(lax.dot_general(table, gradient, (((0,), (0,)), ((), ())...  29.1 us
    ppermute x8, waiting for transfers between devices, padded_2(): after = lax.ppermute(leading, axis, down)  22.3 us
    div x2, other arithmetic, relax(): return (rhs + x_weights * near_x + y_weights * near_y) / diagonal_sum  16.9 us
    ppermute x8, starting transfers between devices, padded_2(): after = lax.ppermute(leading, axis, down)  10.5 us
  transfers between devices with their start and end apart: 18, of which 10 were waited for; matrix products, arithmetic and copies ran while one was open for 1% of the time, Pallas kernels for 0%

commit v1 on v0

v1 whole, which is shorter than its diff:
```python
import functools

import jax
import jax.numpy as jnp
from jax import lax
from jax.experimental import pallas as pl
from jax.experimental.pallas import tpu as pltpu
from jax.sharding import PartitionSpec as P

SWEEPS = 3
ROWS = 16
LT = 128
MESH = pl.DeviceIdType.MESH
F32 = jnp.float32
BF16 = jnp.bfloat16


def ew_shift(block, width):
    left = pltpu.roll(block, 1, 1)[:, LT : LT + width]
    right = pltpu.roll(block, block.shape[1] - 1, 1)[:, LT : LT + width]
    return left, right


def ns_shift(block, rows):
    up = pltpu.roll(block, 1, 0)[8 : 8 + rows]
    down = pltpu.roll(block, block.shape[0] - 1, 0)[8 : 8 + rows]
    return up, down


def kernel(
    ngx, ngy,
    vel_h, obs_h, thick_h, rate_h, fric_h, mask_h, codes_h, mx_h, my_h,
    adj_h, coef_ref,
    vel, obs, thick, rate, fric, mask, codes, mx, my,
    s_pad, q1, q2, p_f, g_f, e_f, adj, grad, mxt, myt, t_hi, t_lo,
    edge_out, edge_in, r_send, r_acc, r_in, half_in, z_out, z_in,
    load_sem, store_sem, halo_send, halo_recv, col_send, col_recv,
    pair_sem, half_send, half_recv, z_send, z_recv,
):
    h, w = thick.shape
    ix, iy = lax.axis_index("gx"), lax.axis_index("gy")
    mid = pl.ds(LT, w)
    body = pl.ds(8, h)

    loads = [
        pltpu.make_async_copy(vel_h, vel.at[:, body, mid], load_sem.at[0]),
        pltpu.make_async_copy(mx_h, mx, load_sem.at[1]),
        pltpu.make_async_copy(my_h, my, load_sem.at[2]),
        pltpu.make_async_copy(thick_h, thick, load_sem.at[3]),
        pltpu.make_async_copy(rate_h, rate, load_sem.at[4]),
        pltpu.make_async_copy(mask_h, mask, load_sem.at[5]),
        pltpu.make_async_copy(fric_h, fric, load_sem.at[6]),
        pltpu.make_async_copy(codes_h, codes, load_sem.at[7]),
        pltpu.make_async_copy(obs_h, obs, load_sem.at[8]),
    ]
    for load in loads:
        load.start()

    barrier = pltpu.get_barrier_semaphore()
    for off in range(1, ngx):
        pl.semaphore_signal(barrier, inc=1, device_id=(lax.rem(ix + off, ngx), iy), device_id_type=MESH)
    for off in range(1, ngy):
        pl.semaphore_signal(barrier, inc=1, device_id=(ix, lax.rem(iy + off, ngy)), device_id_type=MESH)
    pl.semaphore_wait(barrier, ngx - 1 + ngy - 1)

    has_n, has_s, has_w, has_e = ix > 0, ix < ngx - 1, iy > 0, iy < ngy - 1

    def row_copies(k, ref):
        down = pltpu.make_async_remote_copy(
            ref.at[:, pl.ds(h, 8), mid], ref.at[:, pl.ds(0, 8), mid],
            halo_send.at[k, 0], halo_recv.at[k, 0], device_id=(ix + 1, iy), device_id_type=MESH)
        up = pltpu.make_async_remote_copy(
            ref.at[:, pl.ds(8, 8), mid], ref.at[:, pl.ds(h + 8, 8), mid],
            halo_send.at[k, 1], halo_recv.at[k, 1], device_id=(ix - 1, iy), device_id_type=MESH)
        return down, up

    def col_copies(k, n):
        east = pltpu.make_async_remote_copy(
            edge_out.at[k, 0, pl.ds(0, n)], edge_in.at[k, 0, pl.ds(0, n)],
            col_send.at[k, 0], col_recv.at[k, 0], device_id=(ix, iy + 1), device_id_type=MESH)
        west = pltpu.make_async_remote_copy(
            edge_out.at[k, 1, pl.ds(0, n)], edge_in.at[k, 1, pl.ds(0, n)],
            col_send.at[k, 1], col_recv.at[k, 1], device_id=(ix, iy - 1), device_id_type=MESH)
        return east, west

    def send_edges(k, ref):
        n = ref.shape[0]
        down, up = row_copies(k, ref)
        east, west = col_copies(k, n)

        @pl.when(has_s)
        def _():
            down.start()

        @pl.when(has_n)
        def _():
            up.start()

        for c in range(n):
            edge_out[k, 0, c] = ref[c, body, pl.ds(w, LT)].T[LT - 8 :]
            edge_out[k, 1, c] = ref[c, body, pl.ds(LT, LT)].T[:8]

        @pl.when(has_e)
        def _():
            east.start()

        @pl.when(has_w)
        def _():
            west.start()

    def take_edges(k, ref):
        n = ref.shape[0]
        down, up = row_copies(k, ref)
        east, west = col_copies(k, n)

        @pl.when(has_w)
        def _():
            east.wait_recv()
            for c in range(n):
                ref[c, body, pl.ds(0, LT)] = jnp.broadcast_to(edge_in[k, 0, c][7:8], (LT, h)).T

        @pl.when(iy == 0)
        def _():
            ref[:, body, pl.ds(0, LT)] = jnp.zeros((n, h, LT), F32)

        @pl.when(has_e)
        def _():
            west.wait_recv()
            for c in range(n):
                ref[c, body, pl.ds(LT + w, LT)] = jnp.broadcast_to(edge_in[k, 1, c][0:1], (LT, h)).T

        @pl.when(iy == ngy - 1)
        def _():
            ref[:, body, pl.ds(LT + w, LT)] = jnp.zeros((n, h, LT), F32)

        @pl.when(has_n)
        def _():
            down.wait_recv()

        @pl.when(ix == 0)
        def _():
            ref[:, pl.ds(0, 8), mid] = jnp.zeros((n, 8, w), F32)

        @pl.when(has_s)
        def _():
            up.wait_recv()

        @pl.when(ix == ngx - 1)
        def _():
            ref[:, pl.ds(h + 8, 8), mid] = jnp.zeros((n, 8, w), F32)

    def drain_edges(k, ref):
        n = ref.shape[0]
        down, up = row_copies(k, ref)
        east, west = col_copies(k, n)
        for there, copy in ((has_s, down), (has_n, up), (has_e, east), (has_w, west)):

            @pl.when(there)
            def _(copy=copy):
                copy.wait_send()

    def over_rows(step):
        def one(i, carry):
            step(pl.multiple_of(i * ROWS, ROWS))
            return carry

        lax.fori_loop(0, h // ROWS, one, 0)

    def neighbours(ref, c, r):
        up, down = ns_shift(ref[c, pl.ds(r, ROWS + 16), mid], ROWS)
        left, right = ew_shift(ref[c, pl.ds(r + 8, ROWS), :], w)
        return up, down, left, right

    loads[0].wait()
    send_edges(0, vel)
    loads[1].wait()
    loads[2].wait()
    mxt[...] = mx[...].T
    myt[...] = my[...].T.reshape(myt.shape)
    for load in loads[3:6]:
        load.wait()
    take_edges(0, vel)

    def viscosity(r):
        up, down, left, right = neighbours(vel, 0, r)
        ux, uy = down - up, right - left
        up, down, left, right = neighbours(vel, 1, r)
        vx, vy = down - up, right - left
        shear = uy + vx
        strain = 0.25 * (ux * ux + vy * vy + ux * vy + 0.25 * (shear * shear))
        here = pl.ds(r, ROWS)
        half = 0.5 * thick[here, :] * rate[here, :]
        root = half * lax.rsqrt(half) * jnp.exp2(jnp.log2(strain + 0.01) * (-1.0 / 6.0))
        s_pad[0, pl.ds(r + 8, ROWS), mid] = jnp.where(mask[here, :] >= 1, root, 0.0)

    over_rows(viscosity)
    send_edges(1, s_pad)
    for load in loads[6:]:
        load.wait()

    def sources(r):
        here, there = pl.ds(r, ROWS), pl.ds(r + 8, ROWS)
        kind = mask[here, :]
        s = s_pad[0, there, mid]
        drag = jnp.where(kind == 2, fric[here, :], 0.0)
        fric[here, :] = drag
        code = codes[here, :] & 15
        pairs = code - (lax.shift_right_logical(code, 1) & 5)
        fronts = ((pairs & 3) + lax.shift_right_logical(pairs, 2)).astype(F32)
        e_f[here, :] = 2.0 * (s * s) * fronts + drag + 1.0
        for c in range(2):
            obs[c, here, :] = jnp.where(kind >= 1, vel[c, there, mid] - obs[c, here, :], 0.0)

    over_rows(sources)
    take_edges(1, s_pad)

    def first(r):
        here, there = pl.ds(r, ROWS), pl.ds(r + 8, ROWS)
        up, down, left, right = neighbours(s_pad, 0, r)
        ns, ew = up + down, left + right
        s = s_pad[0, there, mid]
        e = e_f[here, :]
        for c, total in ((0, 4.0 * ns + ew), (1, ns + 4.0 * ew)):
            inverse = 1.0 / (s * total + e)
            value = obs[c, here, :] * inverse
            p_f[c, here, :] = value
            g_f[c, here, :] = s * inverse
            q1[c, there, mid] = s * value

    over_rows(first)
    send_edges(2, q1)
    take_edges(2, q1)

    def weighted(ref, c, r):
        up, down, left, right = neighbours(ref, c, r)
        ns, ew = up + down, left + right
        return 4.0 * ns + ew if c == 0 else ns + 4.0 * ew

    def second(r):
        here, there = pl.ds(r, ROWS), pl.ds(r + 8, ROWS)
        s = s_pad[0, there, mid]
        for c in range(2):
            total = weighted(q1, c, r)
            q2[c, there, mid] = q1[c, there, mid] + s * g_f[c, here, :] * total

    over_rows(second)
    send_edges(3, q2)
    take_edges(3, q2)

    def third(r):
        here, there = pl.ds(r, ROWS), pl.ds(r + 8, ROWS)
        flux = None
        for c in range(2):
            value = p_f[c, here, :] + g_f[c, here, :] * weighted(q2, c, r)
            adj[c, here, :] = value
            term = vel[c, there, mid] * value
            flux = term if flux is None else flux + term
        grad[here, :] = (-fric[here, :] * flux).astype(BF16)

    over_rows(third)
    store = pltpu.make_async_copy(adj, adj_h, store_sem)
    store.start()

    table = jnp.dot(mxt[...], grad[...], preferred_element_type=F32)
    high = table.astype(BF16)
    t_hi[...] = high
    t_lo[...] = (table - high.astype(F32)).astype(BF16)

    nblk, kb, km = r_acc.shape
    core = lax.rem(iy, 2)

    def project(side):
        rows = myt[:, side].reshape(nblk * kb, h)
        dims = (((1,), (1,)), ((), ()))
        out = lax.dot_general(rows, t_hi[...], dims, preferred_element_type=F32)
        out = out + lax.dot_general(rows, t_lo[...], dims, preferred_element_type=F32)
        return out.reshape(nblk, kb, km)

    r_send[...] = project(1 - core)
    pair = pltpu.make_async_remote_copy(
        r_send, r_in, pair_sem.at[0], pair_sem.at[1],
        device_id=(ix, iy + 1 - 2 * core), device_id_type=MESH)
    pair.start()
    r_acc[...] = project(core)
    pair.wait_recv()
    r_acc[...] += r_in[...]

    nbits = nblk.bit_length() - 1
    hw = km // 2
    cell = iy // 2
    bits = [lax.rem(cell // (1 << t), 2) for t in range(nbits)]
    sent = []
    live = [dict(), dict()]
    slot = 0
    for stage in range(nbits):
        flying = []
        for half in range(2):
            t = stage if half == 0 else nbits - 1 - stage
            free = [b for b in range(nbits) if b not in live[half] and b != t]
            lanes = pl.ds(half * hw, hw)
            for combo in range(1 << len(free)):
                fixed = sum(((combo >> n) & 1) << b for n, b in enumerate(free))
                fixed = fixed + sum((bits[b] * (1 << b) for b in live[half]), 0)
                src = fixed + (1 - bits[t]) * (1 << t)
                dst = fixed + bits[t] * (1 << t)
                copy = pltpu.make_async_remote_copy(
                    r_acc.at[src, :, lanes], half_in.at[slot],
                    half_send.at[slot], half_recv.at[slot],
                    device_id=(ix, iy + (1 - 2 * bits[t]) * (2 << t)), device_id_type=MESH)
                copy.start()
                flying.append((copy, dst, lanes, slot))
                slot += 1
            live[half][t] = True
        for copy, dst, lanes, place in flying:
            copy.wait_recv()
            r_acc[dst, :, lanes] += half_in[place]
            sent.append(copy)

    ab = km // ngx
    for d in range(ngx):
        z_out[d] = r_acc[cell, :, d * ab : (d + 1) * ab]
    copies = []
    for off in range(1, ngx):
        to = lax.rem(ix + off, ngx)
        copy = pltpu.make_async_remote_copy(
            z_out.at[to], z_in.at[off - 1], z_send.at[off - 1], z_recv.at[off - 1],
            device_id=(to, iy), device_id_type=MESH)
        copy.start()
        copies.append(copy)
    total = z_out[ix]
    for off, copy in enumerate(copies):
        copy.wait_recv()
        total = total + z_in[off]
    coef_ref[...] = total.T

    for copy in copies + sent + [pair]:
        copy.wait_send()
    for k, ref in enumerate((vel, s_pad, q1, q2)):
        drain_edges(k, ref)
    store.wait()


def shards(ngx, ngy, velocity, observed, thickness, rate_factor, friction, cell_mask, front_codes, modes_x, modes_y):
    h, w = thickness.shape
    km = modes_x.shape[1]
    nblk, kb, ab = ngy // 2, km // ngy, km // ngx
    slots = 2 * sum(nblk >> (t + 1) for t in range(nblk.bit_length() - 1))
    any_spec = pl.BlockSpec(memory_space=pl.ANY)
    pad = (h + 16, w + 2 * LT)
    dma = pltpu.SemaphoreType.DMA
    return pl.pallas_call(
        functools.partial(kernel, ngx, ngy),
        out_shape=(
            jax.ShapeDtypeStruct((2, h, w), F32),
            jax.ShapeDtypeStruct((ab, kb), F32),
        ),
        in_specs=[any_spec] * 9,
        out_specs=(any_spec, pl.BlockSpec(memory_space=pltpu.VMEM)),
        scratch_shapes=[
            pltpu.VMEM((2, *pad), F32),
            pltpu.VMEM((2, h, w), F32),
            pltpu.VMEM((h, w), F32),
            pltpu.VMEM((h, w), F32),
            pltpu.VMEM((h, w), F32),
            pltpu.VMEM((h, w), jnp.int32),
            pltpu.VMEM((h, w), jnp.int32),
            pltpu.VMEM((h, km), BF16),
            pltpu.VMEM((w, km), BF16),
            pltpu.VMEM((1, *pad), F32),
            pltpu.VMEM((2, *pad), F32),
            pltpu.VMEM((2, *pad), F32),
            pltpu.VMEM((2, h, w), F32),
            pltpu.VMEM((2, h, w), F32),
            pltpu.VMEM((h, w), F32),
            pltpu.VMEM((2, h, w), F32),
            pltpu.VMEM((h, w), BF16),
            pltpu.VMEM((km, h), BF16),
            pltpu.VMEM((nblk, 2, kb, w), BF16),
            pltpu.VMEM((km, w), BF16),
            pltpu.VMEM((km, w), BF16),
            pltpu.VMEM((4, 2, 2, 8, h), F32),
            pltpu.VMEM((4, 2, 2, 8, h), F32),
            pltpu.VMEM((nblk, kb, km), F32),
            pltpu.VMEM((nblk, kb, km), F32),
            pltpu.VMEM((nblk, kb, km), F32),
            pltpu.VMEM((slots, kb, km // 2), F32),
            pltpu.VMEM((ngx, kb, ab), F32),
            pltpu.VMEM((ngx - 1, kb, ab), F32),
            dma((9,)),
            dma,
            dma((4, 2)),
            dma((4, 2)),
            dma((4, 2)),
            dma((4, 2)),
            dma((2,)),
            dma((slots,)),
            dma((slots,)),
            dma((ngx - 1,)),
            dma((ngx - 1,)),
        ],
        compiler_params=pltpu.CompilerParams(
            collective_id=0, has_side_effects=True, vmem_limit_bytes=56 * 1024 * 1024
        ),
    )(velocity, observed, thickness, rate_factor, friction, cell_mask, front_codes, modes_x, modes_y)


def solution(mesh):
    tile = P("gx", "gy")
    pair = P(None, "gx", "gy")
    return jax.shard_map(
        functools.partial(shards, mesh.shape["gx"], mesh.shape["gy"]),
        mesh=mesh,
        in_specs=(pair, pair, tile, tile, tile, tile, tile, P("gx", None), P("gy", None)),
        out_specs=(pair, tile),
        check_vma=False,
    )
```

time: 192 us -> 54 us (0.28)
  waiting for transfers between devices: 87.2 us -> 0 us
  Pallas kernels: 0 us -> 48.5 us
  starting transfers between devices: 41.6 us -> 0 us
  other arithmetic: 33.4 us -> 0 us
  between operations: 14.5 us -> 0.64 us
  local copies, waits for them, and re-layouts: 11.4 us -> 4.62 us
  matrix products: 3.42 us -> 0 us
    pallas_call x0 -> x1, Pallas kernels: none -> 48.5 us  [shards(): pl.pallas_call(functools.partial(kernel, ngx, ngy), out_shape=(jax.ShapeD...]
    ppermute x16 -> x0, starting transfers between devices: 41.5 us -> none  [the longest x8 31 us: padded_2(): before = lax.ppermute(last, axis, up)]
    unnamed x3 -> x0, waiting for transfers between devices: 33.9 us -> none
    reduce_scatter x1 -> x0, waiting for transfers between devices: 29.1 us -> none  [shards(): lax.psum_scatter(lax.dot_general(table, gradient, (((0,), (0,)), ((), ())...]
    ppermute x16 -> x0, waiting for transfers between devices: 24.1 us -> none  [the longest x8 22.3 us: padded_2(): after = lax.ppermute(leading, axis, down)]
    div x3 -> x0, other arithmetic: 19.4 us -> none  [the longest x2 16.9 us: relax(): return (rhs + x_weights * near_x + y_weights * near_y) / diagonal_sum]
    add x2 -> x0, other arithmetic: 5.87 us -> none  [the longest x1 3.48 us: shards(): lower_x + upper_x]
    slice x10 -> x0, local copies, waits for them, and re-layouts: 5.29 us -> none  [the longest x6 2.76 us: padded_2(): last = lax.slice_in_dim(array, length - width, length, axis=dim)]
  transfers between devices with their start and end apart: 18 -> 0, of which waited for: 10 -> 0; matrix products, arithmetic and copies ran while one was open for 1% -> 0% of each run, Pallas kernels for 0% -> 0%
where the time goes in v1:
time: 54 us; the launch traced here: 53.8 us
  Pallas kernels  48.5 us (90%)
  local copies, waits for them, and re-layouts  4.62 us (9%)
  between operations  0.64 us (1%)
    pallas_call x1, Pallas kernels, shards(): pl.pallas_call(functools.partial(kernel, ngx, ngy), out_shape=(jax.ShapeD...  48.5 us
    unnamed x1, local copies, waits for them, and re-layouts  3.08 us
    pallas_call x1, local copies, waits for them, and re-layouts, shards(): pl.pallas_call(functools.partial(kernel, ngx, ngy), out_shape=(jax.ShapeD...  1.54 us

profile of v1, /device:TPU:0, one launch (start us, length us, event | category | flops | bytes accessed | tf_op | source)
XLA Modules:
  0.0 53.8 jit_solution(5558179893254470585)
XLA Ops:
  0.6 48.5 %shard_map.104 = (f32[2,512,512]{2,1,0:T(8,128)}, f32[128,64]{1,0:T(8,128)}) custom-call(f32[2,512,512]{2,1,0:T(8,128)} %vel_h.1, f32[2,512,512]{2,1,0:T(8,128)} %obs_h.1, f32[512,512]{1,0:T(8,128)} %thick_h.1, f32[512,512]{1,0:T(8,128)} %rate_h.1, f32[512,512]{1,0:T(8,128)} %fric_h.1, s32[512,512]{1,0:T(8,128)} %mask_h.1, s32[512,512]{1,0:T(8,128)} %codes_h.1, ...), custom_call_target="tpu_custom_call" | custom-call | tf_op jit(solution)/shard_map/pallas_call | solution.py:351
  49.2 1.5 %copy.11 = f32[128,64]{0,1:T(8,128)} copy(f32[128,64]{1,0:T(8,128)} %get-tuple-element.3) | data formatting | bytes 65536 | tf_op jit(solution)/shard_map/pallas_call | solution.py:351
  50.7 3.1 %copy.13 = f32[2,512,512]{2,1,0:T(8,128)} copy(f32[2,512,512]{2,1,0:T(8,128)} %get-tuple-element.6) | data formatting | bytes 4194304

commit v2 on v1

v2 whole, which is shorter than its diff:
```python
import functools

import jax
import jax.numpy as jnp
from jax import lax
from jax.experimental import pallas as pl
from jax.experimental.pallas import tpu as pltpu
from jax.sharding import PartitionSpec as P

SWEEPS = 3
ROWS = 32
LT = 128
VMEM_LIMIT = 48 * 1024 * 1024
MESH = pl.DeviceIdType.MESH
F32 = jnp.float32
BF16 = jnp.bfloat16


def kernel(
    ngx, ngy,
    vel_h, obs_h, thick_h, rate_h, fric_h, mask_h, codes_h, mx_h, my_h,
    adj, coef_ref,
    vel, obs, thick, rate, fric, mask, codes, mx, my,
    s_pad, q1, q2, p_f, g_f, e_f, grad, mxt, myt, t_hi, t_lo,
    edge_out, edge_in, halo, r_send, r_acc, r_in, half_in, z_out, z_in,
    vel_sem, load_sem, halo_send, halo_recv, col_send, col_recv,
    pair_sem, half_send, half_recv, z_send, z_recv,
):
    h, w = thick.shape
    nt = w // LT
    ix, iy = lax.axis_index("gx"), lax.axis_index("gy")
    body = pl.ds(8, h)
    outer, inner = (0, nt - 1), tuple(range(1, nt - 1))

    vel_loads = [
        pltpu.make_async_copy(
            vel_h.at[:, :, pl.ds(t * LT, LT)], vel.at[:, t, body], vel_sem.at[t])
        for t in outer + inner
    ]
    loads = [
        pltpu.make_async_copy(thick_h, thick, load_sem.at[0]),
        pltpu.make_async_copy(rate_h, rate, load_sem.at[1]),
        pltpu.make_async_copy(mask_h, mask, load_sem.at[2]),
        pltpu.make_async_copy(fric_h, fric, load_sem.at[3]),
        pltpu.make_async_copy(codes_h, codes, load_sem.at[4]),
        pltpu.make_async_copy(obs_h, obs, load_sem.at[5]),
        pltpu.make_async_copy(mx_h, mx, load_sem.at[6]),
        pltpu.make_async_copy(my_h, my, load_sem.at[7]),
    ]
    for load in vel_loads + loads:
        load.start()

    barrier = pltpu.get_barrier_semaphore()
    for off in range(1, ngx):
        pl.semaphore_signal(barrier, inc=1, device_id=(lax.rem(ix + off, ngx), iy), device_id_type=MESH)
    for off in range(1, ngy):
        pl.semaphore_signal(barrier, inc=1, device_id=(ix, lax.rem(iy + off, ngy)), device_id_type=MESH)
    pl.semaphore_wait(barrier, ngx - 1 + ngy - 1)

    has_n, has_s, has_w, has_e = ix > 0, ix < ngx - 1, iy > 0, iy < ngy - 1

    fields = (vel, s_pad, q1, q2)

    for missing, rows in ((ix == 0, 0), (ix == ngx - 1, h + 8)):

        @pl.when(missing)
        def _(rows=rows):
            for ref in fields:
                ref[:, :, pl.ds(rows, 8)] = jnp.zeros((ref.shape[0], nt, 8, LT), F32)

    for missing, side in ((iy == 0, 0), (iy == ngy - 1, 1)):

        @pl.when(missing)
        def _(side=side):
            edge_in[:, side] = jnp.zeros((4, 8, h), F32)

    def copies_of(k):
        ref = fields[k]
        down = pltpu.make_async_remote_copy(
            ref.at[:, :, pl.ds(h, 8)], ref.at[:, :, pl.ds(0, 8)],
            halo_send.at[k, 0], halo_recv.at[k, 0], device_id=(ix + 1, iy), device_id_type=MESH)
        up = pltpu.make_async_remote_copy(
            ref.at[:, :, pl.ds(8, 8)], ref.at[:, :, pl.ds(h + 8, 8)],
            halo_send.at[k, 1], halo_recv.at[k, 1], device_id=(ix - 1, iy), device_id_type=MESH)
        east = pltpu.make_async_remote_copy(
            edge_out.at[k], edge_in.at[k, 0],
            col_send.at[k, 0], col_recv.at[k, 0], device_id=(ix, iy + 1), device_id_type=MESH)
        west = pltpu.make_async_remote_copy(
            edge_out.at[k], edge_in.at[k, 1],
            col_send.at[k, 1], col_recv.at[k, 1], device_id=(ix, iy - 1), device_id_type=MESH)
        return (has_s, down), (has_n, up), (has_e, east), (has_w, west)

    def start(there, copy):
        @pl.when(there)
        def _():
            copy.start()

    def send_rows(k):
        for there, copy in copies_of(k)[:2]:
            start(there, copy)

    def send_columns(k):
        ref = fields[k]
        lane = lax.broadcasted_iota(jnp.int32, (h, LT), 1)
        pack = pltpu.roll(ref[0, nt - 1, body], 1, 1)
        pack = jnp.where(lane == 7, pltpu.roll(ref[0, 0, body], 7, 1), pack)
        if ref.shape[0] == 2:
            pack = jnp.where(lane == 1, pltpu.roll(ref[1, nt - 1, body], 2, 1), pack)
            pack = jnp.where(lane == 6, pltpu.roll(ref[1, 0, body], 6, 1), pack)
        edge_out[k] = pack.T[:8]
        for there, copy in copies_of(k)[2:]:
            start(there, copy)

    def take_edges(k):
        (_, down), (_, up), (_, east), (_, west) = copies_of(k)
        for there, copy in ((has_w, east), (has_e, west), (has_n, down), (has_s, up)):

            @pl.when(there)
            def _(copy=copy):
                copy.wait_recv()

        row = lax.broadcasted_iota(jnp.int32, (8, h), 0)
        both = jnp.where(row < 4, edge_in[k, 0], edge_in[k, 1])
        halo[k] = jnp.concatenate([both] * (LT // 8), axis=0).T

    def drain_edges(k):
        for there, copy in copies_of(k):

            @pl.when(there)
            def _(copy=copy):
                copy.wait_send()

    def rows_of(step, first, last, stride=ROWS):
        def one(i, carry):
            step(pl.multiple_of(first + i * stride, ROWS))
            return carry

        lax.fori_loop(0, (last - first) // stride, one, 0)

    def border(step):
        rows_of(lambda r: step(r, outer), 0, h)
        rows_of(lambda r: step(r, inner), 0, 2 * (h - ROWS), h - ROWS)

    def interior(step):
        rows_of(lambda r: step(r, inner), ROWS, h - ROWS)

    lanes = lax.broadcasted_iota(jnp.int32, (ROWS, LT), 1)
    at_first, at_last = lanes == 0, lanes == LT - 1

    def cols(t):
        return pl.ds(t * LT, LT)

    def neighbours(k, c, r, t, kept):
        ref = fields[k]

        def turned(tile, by):
            if (c, tile, by) not in kept:
                kept[c, tile, by] = pltpu.roll(ref[c, tile, pl.ds(r + 8, ROWS)], by, 1)
            return kept[c, tile, by]

        def edge(by):
            value = halo[k, pl.ds(r, ROWS)]
            return pltpu.roll(value, by, 1) if c else value

        up = ref[c, t, pl.ds(r + 7, ROWS)]
        down = ref[c, t, pl.ds(r + 9, ROWS)]
        before = turned(t - 1, 1) if t else edge(LT - 1)
        after = turned(t + 1, LT - 1) if t < nt - 1 else edge(1)
        left = jnp.where(at_first, before, turned(t, 1))
        right = jnp.where(at_last, after, turned(t, LT - 1))
        return up, down, left, right

    def weighted(k, c, r, t, kept):
        up, down, left, right = neighbours(k, c, r, t, kept)
        ns, ew = up + down, left + right
        return 4.0 * ns + ew if c == 0 else ns + 4.0 * ew

    def viscosity(r, tiles):
        kept = {}
        for t in tiles:
            up, down, left, right = neighbours(0, 0, r, t, kept)
            ux, uy = down - up, right - left
            up, down, left, right = neighbours(0, 1, r, t, kept)
            vx, vy = down - up, right - left
            shear = uy + vx
            strain = 0.25 * (ux * ux + vy * vy + ux * vy + 0.25 * (shear * shear))
            here = pl.ds(r, ROWS)
            half = 0.5 * thick[here, cols(t)] * rate[here, cols(t)]
            root = half * lax.rsqrt(half) * jnp.exp2(jnp.log2(strain + 0.01) * (-1.0 / 6.0))
            s_pad[0, t, pl.ds(r + 8, ROWS)] = jnp.where(mask[here, cols(t)] >= 1, root, 0.0)

    def sources(r, tiles):
        here, there = pl.ds(r, ROWS), pl.ds(r + 8, ROWS)
        for t in tiles:
            kind = mask[here, cols(t)]
            s = s_pad[0, t, there]
            drag = jnp.where(kind == 2, fric[here, cols(t)], 0.0)
            fric[here, cols(t)] = drag
            code = codes[here, cols(t)] & 15
            pairs = code - (lax.shift_right_logical(code, 1) & 5)
            fronts = ((pairs & 3) + lax.shift_right_logical(pairs, 2)).astype(F32)
            e_f[here, cols(t)] = 2.0 * (s * s) * fronts + drag + 1.0
            for c in range(2):
                obs[c, here, cols(t)] = jnp.where(kind >= 1, vel[c, t, there] - obs[c, here, cols(t)], 0.0)

    def first(r, tiles):
        here, there = pl.ds(r, ROWS), pl.ds(r + 8, ROWS)
        kept = {}
        for t in tiles:
            up, down, left, right = neighbours(1, 0, r, t, kept)
            ns, ew = up + down, left + right
            s = s_pad[0, t, there]
            e = e_f[here, cols(t)]
            for c, total in ((0, 4.0 * ns + ew), (1, ns + 4.0 * ew)):
                inverse = 1.0 / (s * total + e)
                value = obs[c, here, cols(t)] * inverse
                p_f[c, here, cols(t)] = value
                g_f[c, here, cols(t)] = s * inverse
                q1[c, t, there] = s * value

    def second(r, tiles):
        here, there = pl.ds(r, ROWS), pl.ds(r + 8, ROWS)
        kept = {}
        for t in tiles:
            s = s_pad[0, t, there]
            for c in range(2):
                total = weighted(2, c, r, t, kept)
                q2[c, t, there] = q1[c, t, there] + s * g_f[c, here, cols(t)] * total

    def third(r, tiles):
        here, there = pl.ds(r, ROWS), pl.ds(r + 8, ROWS)
        kept = {}
        for t in tiles:
            flux = None
            for c in range(2):
                value = p_f[c, here, cols(t)] + g_f[c, here, cols(t)] * weighted(3, c, r, t, kept)
                adj[c, here, cols(t)] = value
                term = vel[c, t, there] * value
                flux = term if flux is None else flux + term
            grad[here, cols(t)] = (-fric[here, cols(t)] * flux).astype(BF16)

    for load in vel_loads:
        load.wait()
    send_rows(0)
    send_columns(0)
    for load in loads[:3]:
        load.wait()
    take_edges(0)
    border(viscosity)
    send_columns(1)
    send_rows(1)
    interior(viscosity)
    for load in loads[3:]:
        load.wait()
    rows_of(lambda r: sources(r, range(nt)), 0, h)
    mxt[...] = mx[...].T
    myt[...] = my[...].T.reshape(myt.shape)
    take_edges(1)
    border(first)
    send_columns(2)
    send_rows(2)
    interior(first)
    take_edges(2)
    border(second)
    send_columns(3)
    send_rows(3)
    interior(second)
    interior(third)
    take_edges(3)
    border(third)

    table = jnp.dot(mxt[...], grad[...], preferred_element_type=F32)
    high = table.astype(BF16)
    t_hi[...] = high
    t_lo[...] = (table - high.astype(F32)).astype(BF16)

    nblk, kb, km = r_acc.shape
    core = lax.rem(iy, 2)

    def project(side):
        rows = myt[:, side].reshape(nblk * kb, h)
        dims = (((1,), (1,)), ((), ()))
        out = lax.dot_general(rows, t_hi[...], dims, preferred_element_type=F32)
        out = out + lax.dot_general(rows, t_lo[...], dims, preferred_element_type=F32)
        return out.reshape(nblk, kb, km)

    r_send[...] = project(1 - core)
    pair = pltpu.make_async_remote_copy(
        r_send, r_in, pair_sem.at[0], pair_sem.at[1],
        device_id=(ix, iy + 1 - 2 * core), device_id_type=MESH)
    pair.start()
    r_acc[...] = project(core)
    pair.wait_recv()
    r_acc[...] += r_in[...]

    nbits = nblk.bit_length() - 1
    hw = km // 2
    cell = iy // 2
    bits = [lax.rem(cell // (1 << t), 2) for t in range(nbits)]
    sent = []
    live = [dict(), dict()]
    slot = 0
    for stage in range(nbits):
        flying = []
        for half in range(2):
            t = stage if half == 0 else nbits - 1 - stage
            free = [b for b in range(nbits) if b not in live[half] and b != t]
            lanes = pl.ds(half * hw, hw)
            for combo in range(1 << len(free)):
                fixed = sum(((combo >> n) & 1) << b for n, b in enumerate(free))
                fixed = fixed + sum((bits[b] * (1 << b) for b in live[half]), 0)
                src = fixed + (1 - bits[t]) * (1 << t)
                dst = fixed + bits[t] * (1 << t)
                copy = pltpu.make_async_remote_copy(
                    r_acc.at[src, :, lanes], half_in.at[slot],
                    half_send.at[slot], half_recv.at[slot],
                    device_id=(ix, iy + (1 - 2 * bits[t]) * (2 << t)), device_id_type=MESH)
                copy.start()
                flying.append((copy, dst, lanes, slot))
                slot += 1
            live[half][t] = True
        for copy, dst, lanes, place in flying:
            copy.wait_recv()
            r_acc[dst, :, lanes] += half_in[place]
            sent.append(copy)

    ab = km // ngx
    for d in range(ngx):
        z_out[d] = r_acc[cell, :, d * ab : (d + 1) * ab]
    copies = []
    for off in range(1, ngx):
        to = lax.rem(ix + off, ngx)
        copy = pltpu.make_async_remote_copy(
            z_out.at[to], z_in.at[off - 1], z_send.at[off - 1], z_recv.at[off - 1],
            device_id=(to, iy), device_id_type=MESH)
        copy.start()
        copies.append(copy)
    total = z_out[ix]
    for off, copy in enumerate(copies):
        copy.wait_recv()
        total = total + z_in[off]
    coef_ref[...] = total

    for copy in copies + sent + [pair]:
        copy.wait_send()
    for k in range(4):
        drain_edges(k)


def write_results(adj, coef, adj_h, coef_h, adj_sem, coef_sem):
    rows = adj.shape[1] // 2
    copies = [pltpu.make_async_copy(coef, coef_h, coef_sem)]
    for n in range(4):
        part = (n % 2, pl.ds(n // 2 * rows, rows))
        copies.append(pltpu.make_async_copy(adj.at[part], adj_h.at[part], adj_sem.at[n]))
    for copy in copies:
        copy.start()
    for copy in copies:
        copy.wait()


def shards(ngx, ngy, velocity, observed, thickness, rate_factor, friction, cell_mask, front_codes, modes_x, modes_y):
    h, w = thickness.shape
    km = modes_x.shape[1]
    nblk, kb, ab = ngy // 2, km // ngy, km // ngx
    slots = 2 * sum(nblk >> (t + 1) for t in range(nblk.bit_length() - 1))
    hbm_spec = pl.BlockSpec(memory_space=pltpu.HBM)
    vmem_spec = pl.BlockSpec(memory_space=pltpu.VMEM)
    pad = (w // LT, h + 16, LT)
    dma = pltpu.SemaphoreType.DMA
    args = (velocity, observed, thickness, rate_factor, friction, cell_mask, front_codes, modes_x, modes_y)
    args = [pltpu.with_memory_space_constraint(x, pltpu.HBM) for x in args]
    adjoint, coefficients = pl.pallas_call(
        functools.partial(kernel, ngx, ngy),
        out_shape=(pltpu.VMEM((2, h, w), F32), pltpu.VMEM((kb, ab), F32)),
        in_specs=[hbm_spec] * 9,
        out_specs=(vmem_spec, vmem_spec),
        scratch_shapes=[
            pltpu.VMEM((2, *pad), F32),
            pltpu.VMEM((2, h, w), F32),
            pltpu.VMEM((h, w), F32),
            pltpu.VMEM((h, w), F32),
            pltpu.VMEM((h, w), F32),
            pltpu.VMEM((h, w), jnp.int32),
            pltpu.VMEM((h, w), jnp.int32),
            pltpu.VMEM((h, km), BF16),
            pltpu.VMEM((w, km), BF16),
            pltpu.VMEM((1, *pad), F32),
            pltpu.VMEM((2, *pad), F32),
            pltpu.VMEM((2, *pad), F32),
            pltpu.VMEM((2, h, w), F32),
            pltpu.VMEM((2, h, w), F32),
            pltpu.VMEM((h, w), F32),
            pltpu.VMEM((h, w), BF16),
            pltpu.VMEM((km, h), BF16),
            pltpu.VMEM((nblk, 2, kb, w), BF16),
            pltpu.VMEM((km, w), BF16),
            pltpu.VMEM((km, w), BF16),
            pltpu.VMEM((4, 8, h), F32),
            pltpu.VMEM((4, 2, 8, h), F32),
            pltpu.VMEM((4, h, LT), F32),
            pltpu.VMEM((nblk, kb, km), F32),
            pltpu.VMEM((nblk, kb, km), F32),
            pltpu.VMEM((nblk, kb, km), F32),
            pltpu.VMEM((slots, kb, km // 2), F32),
            pltpu.VMEM((ngx, kb, ab), F32),
            pltpu.VMEM((ngx - 1, kb, ab), F32),
            dma((w // LT,)),
            dma((8,)),
            dma((4, 2)),
            dma((4, 2)),
            dma((4, 2)),
            dma((4, 2)),
            dma((2,)),
            dma((slots,)),
            dma((slots,)),
            dma((ngx - 1,)),
            dma((ngx - 1,)),
        ],
        compiler_params=pltpu.CompilerParams(
            collective_id=0, has_side_effects=True, vmem_limit_bytes=VMEM_LIMIT
        ),
    )(*args)
    adjoint = pltpu.with_memory_space_constraint(adjoint, pltpu.VMEM)
    coefficients = pltpu.with_memory_space_constraint(coefficients, pltpu.VMEM)
    adjoint, coefficients = pl.pallas_call(
        write_results,
        out_shape=(
            jax.ShapeDtypeStruct((2, h, w), F32),
            jax.ShapeDtypeStruct((kb, ab), F32),
        ),
        in_specs=[vmem_spec, vmem_spec],
        out_specs=(hbm_spec, hbm_spec),
        scratch_shapes=[dma((4,)), dma],
    )(adjoint, coefficients)
    return adjoint, coefficients.T


def solution(mesh):
    tile = P("gx", "gy")
    pair = P(None, "gx", "gy")
    return jax.shard_map(
        functools.partial(shards, mesh.shape["gx"], mesh.shape["gy"]),
        mesh=mesh,
        in_specs=(pair, pair, tile, tile, tile, tile, tile, P("gx", None), P("gy", None)),
        out_specs=(pair, tile),
        check_vma=False,
    )
```

time: 54 us -> 46.7 us (0.86)
  local copies, waits for them, and re-layouts: 4.62 us -> 0 us
  Pallas kernels: 48.5 us -> 45.9 us
    unnamed x1 -> x0, local copies, waits for them, and re-layouts: 3.08 us -> none
    pallas_call x1 -> x2, Pallas kernels: 48.5 us -> 45.9 us  [the longest x1 44.5 us: shards(): pl.pallas_call(functools.partial(kernel, ngx, ngy), out_shape=(pltpu.VMEM...]
    pallas_call x1 -> x0, local copies, waits for them, and re-layouts: 1.54 us -> none  [shards(): pl.pallas_call(functools.partial(kernel, ngx, ngy), out_shape=(jax.ShapeD...]
where the time goes in v2:
time: 46.7 us; the launch traced here: 46.5 us
  Pallas kernels  45.9 us (98%)
  between operations  0.64 us (1%)
    pallas_call x1, Pallas kernels, shards(): pl.pallas_call(functools.partial(kernel, ngx, ngy), out_shape=(pltpu.VMEM...  44.5 us
    pallas_call x1, Pallas kernels, shards(): pl.pallas_call(write_results, out_shape=(jax.ShapeDtypeStruct((2, h, w),...  1.37 us

profile of v2, /device:TPU:0, one launch (start us, length us, event | category | flops | bytes accessed | tf_op | source)
XLA Modules:
  0.0 46.5 jit_solution(16631041165043001993)
XLA Ops:
  0.6 44.5 %shard_map.104 = (f32[2,512,512]{2,1,0:T(8,128)S(1)}, f32[64,128]{1,0:T(8,128)S(1)}) custom-call(f32[2,512,512]{2,1,0:T(8,128)} %vel_h.1, f32[2,512,512]{2,1,0:T(8,128)} %obs_h.1, f32[512,512]{1,0:T(8,128)} %thick_h.1, f32[512,512]{1,0:T(8,128)} %rate_h.1, f32[512,512]{1,0:T(8,128)} %fric_h.1, s32[512,512]{1,0:T(8,128)} %mask_h.1, s32[512,512]{1,0:T(8,128)} %codes_h.1, ...), custom_call_target="tpu_custom_call" | custom-call | tf_op jit(solution)/shard_map/pallas_call | solution.py:373
  45.1 1.4 %shard_map.105 = (f32[2,512,512]{2,1,0:T(8,128)}, f32[64,128]{1,0:T(8,128)}) custom-call(f32[2,512,512]{2,1,0:T(8,128)S(1)} %get-tuple-element.6.adj, f32[64,128]{1,0:T(8,128)S(1)} %get-tuple-element.7.coef), custom_call_target="tpu_custom_call" | custom-call | tf_op jit(solution)/shard_map/pallas_call | solution.py:426

commit v3 on v2

--- a/solution.py
+++ b/solution.py
@@ -8,7 +8,7 @@
 from jax.sharding import PartitionSpec as P
 
 SWEEPS = 3
-ROWS = 32
+ROWS = 64
 LT = 128
 VMEM_LIMIT = 48 * 1024 * 1024
 MESH = pl.DeviceIdType.MESH
@@ -24,7 +24,7 @@
     s_pad, q1, q2, p_f, g_f, e_f, grad, mxt, myt, t_hi, t_lo,
     edge_out, edge_in, halo, r_send, r_acc, r_in, half_in, z_out, z_in,
     vel_sem, load_sem, halo_send, halo_recv, col_send, col_recv,
-    pair_sem, half_send, half_recv, z_send, z_recv,
+    pair_send, pair_recv, half_send, half_recv, z_send, z_recv,
 ):
     h, w = thick.shape
     nt = w // LT
@@ -135,7 +135,7 @@
             step(pl.multiple_of(first + i * stride, ROWS))
             return carry
 
-        lax.fori_loop(0, (last - first) // stride, one, 0)
+        lax.fori_loop(0, (last - first) // stride, one, 0, unroll=2)
 
     def border(step):
         rows_of(lambda r: step(r, outer), 0, h)
@@ -269,79 +269,97 @@
     take_edges(3)
     border(third)
 
-    table = jnp.dot(mxt[...], grad[...], preferred_element_type=F32)
-    high = table.astype(BF16)
-    t_hi[...] = high
-    t_lo[...] = (table - high.astype(F32)).astype(BF16)
-
     nblk, kb, km = r_acc.shape
+    npc, ab = km // LT, km // ngx
     core = lax.rem(iy, 2)
-
-    def project(side):
-        rows = myt[:, side].reshape(nblk * kb, h)
-        dims = (((1,), (1,)), ((), ()))
-        out = lax.dot_general(rows, t_hi[...], dims, preferred_element_type=F32)
-        out = out + lax.dot_general(rows, t_lo[...], dims, preferred_element_type=F32)
-        return out.reshape(nblk, kb, km)
-
-    r_send[...] = project(1 - core)
-    pair = pltpu.make_async_remote_copy(
-        r_send, r_in, pair_sem.at[0], pair_sem.at[1],
-        device_id=(ix, iy + 1 - 2 * core), device_id_type=MESH)
-    pair.start()
-    r_acc[...] = project(core)
-    pair.wait_recv()
-    r_acc[...] += r_in[...]
-
+    cell = iy // 2
     nbits = nblk.bit_length() - 1
-    hw = km // 2
-    cell = iy // 2
     bits = [lax.rem(cell // (1 << t), 2) for t in range(nbits)]
+    rows_dims = (((1,), (1,)), ((), ()))
     sent = []
-    live = [dict(), dict()]
+
+    def project(side, p):
+        rows = myt[:, side].reshape(nblk * kb, w)
+        out = lax.dot_general(rows, t_hi[p], rows_dims, preferred_element_type=F32)
+        out = out + lax.dot_general(rows, t_lo[p], rows_dims, preferred_element_type=F32)
+        return out.reshape(nblk, kb, LT)
+
+    pairs = []
+    for p in range(npc):
+        table = jnp.dot(mxt[p * LT : (p + 1) * LT, :], grad[...], preferred_element_type=F32)
+        high = table.astype(BF16)
+        t_hi[p] = high
+        t_lo[p] = (table - high.astype(F32)).astype(BF16)
+        r_send[p] = project(1 - core, p)
+        pair = pltpu.make_async_remote_copy(
+            r_send.at[p], r_in.at[p], pair_send.at[p], pair_recv.at[p],
+            device_id=(ix, iy + 1 - 2 * core), device_id_type=MESH)
+        pair.start()
+        pairs.append(pair)
+    for p in range(npc):
+        r_acc[:, :, p * LT : (p + 1) * LT] = project(core, p)
+
+    live = [[] for _ in range(npc)]
+    flying = [[] for _ in range(npc)]
     slot = 0
-    for stage in range(nbits):
-        flying = []
-        for half in range(2):
-            t = stage if half == 0 else nbits - 1 - stage
-            free = [b for b in range(nbits) if b not in live[half] and b != t]
-            lanes = pl.ds(half * hw, hw)
-            for combo in range(1 << len(free)):
-                fixed = sum(((combo >> n) & 1) << b for n, b in enumerate(free))
-                fixed = fixed + sum((bits[b] * (1 << b) for b in live[half]), 0)
-                src = fixed + (1 - bits[t]) * (1 << t)
-                dst = fixed + bits[t] * (1 << t)
-                copy = pltpu.make_async_remote_copy(
-                    r_acc.at[src, :, lanes], half_in.at[slot],
-                    half_send.at[slot], half_recv.at[slot],
-                    device_id=(ix, iy + (1 - 2 * bits[t]) * (2 << t)), device_id_type=MESH)
-                copy.start()
-                flying.append((copy, dst, lanes, slot))
-                slot += 1
-            live[half][t] = True
-        for copy, dst, lanes, place in flying:
-            copy.wait_recv()
-            r_acc[dst, :, lanes] += half_in[place]
-            sent.append(copy)
-
-    ab = km // ngx
+    for stage in range(nbits + 1):
+        for p in range(npc):
+            lanes = pl.ds(p * LT, LT)
+            if stage == 0:
+                pairs[p].wait_recv()
+                r_acc[:, :, lanes] += r_in[p]
+                sent.append(pairs[p])
+            for copy, dst, place in flying[p]:
+                copy.wait_recv()
+                r_acc[dst, :, lanes] += half_in[place]
+                sent.append(copy)
+            flying[p] = []
+            if stage < nbits:
+                t = nbits - 1 - stage if p % 2 else stage
+                free = [b for b in range(nbits) if b not in live[p] and b != t]
+                for combo in range(1 << len(free)):
+                    fixed = sum(((combo >> n) & 1) << b for n, b in enumerate(free))
+                    fixed = fixed + sum((bits[b] * (1 << b) for b in live[p]), 0)
+                    src = fixed + (1 - bits[t]) * (1 << t)
+                    dst = fixed + bits[t] * (1 << t)
+                    copy = pltpu.make_async_remote_copy(
+                        r_acc.at[src, :, lanes], half_in.at[slot],
+                        half_send.at[slot], half_recv.at[slot],
+                        device_id=(ix, iy + (1 - 2 * bits[t]) * (2 << t)), device_id_type=MESH)
+                    copy.start()
+                    flying[p].append((copy, dst, slot))
+                    slot += 1
+                live[p].append(t)
+            else:
+                for d in range(p * LT // ab, (p + 1) * LT // ab):
+                    z_out[d] = r_acc[cell, :, d * ab : (d + 1) * ab]
+
+                    @pl.when(ix != d)
+                    def _(d=d):
+                        pltpu.make_async_remote_copy(
+                            z_out.at[d], z_in.at[ix], z_send.at[d], z_recv.at[ix],
+                            device_id=(d, iy), device_id_type=MESH).start()
+
+    def z_copy(d):
+        return pltpu.make_async_remote_copy(
+            z_out.at[d], z_in.at[d], z_send.at[d], z_recv.at[d],
+            device_id=(d, iy), device_id_type=MESH)
+
+    coef_ref[...] = z_out[ix]
     for d in range(ngx):
-        z_out[d] = r_acc[cell, :, d * ab : (d + 1) * ab]
-    copies = []
-    for off in range(1, ngx):
-        to = lax.rem(ix + off, ngx)
-        copy = pltpu.make_async_remote_copy(
-            z_out.at[to], z_in.at[off - 1], z_send.at[off - 1], z_recv.at[off - 1],
-            device_id=(to, iy), device_id_type=MESH)
-        copy.start()
-        copies.append(copy)
-    total = z_out[ix]
-    for off, copy in enumerate(copies):
-        copy.wait_recv()
-        total = total + z_in[off]
-    coef_ref[...] = total
-
-    for copy in copies + sent + [pair]:
+
+        @pl.when(ix != d)
+        def _(d=d):
+            z_copy(d).wait_recv()
+            coef_ref[...] += z_in[d]
+
+    for d in range(ngx):
+
+        @pl.when(ix != d)
+        def _(d=d):
+            z_copy(d).wait_send()
+
+    for copy in sent:
         copy.wait_send()
     for k in range(4):
         drain_edges(k)
@@ -363,7 +381,8 @@
     h, w = thickness.shape
     km = modes_x.shape[1]
     nblk, kb, ab = ngy // 2, km // ngy, km // ngx
-    slots = 2 * sum(nblk >> (t + 1) for t in range(nblk.bit_length() - 1))
+    npc = km // LT
+    slots = npc * sum(nblk >> (t + 1) for t in range(nblk.bit_length() - 1))
     hbm_spec = pl.BlockSpec(memory_space=pltpu.HBM)
     vmem_spec = pl.BlockSpec(memory_space=pltpu.VMEM)
     pad = (w // LT, h + 16, LT)
@@ -394,28 +413,29 @@
             pltpu.VMEM((h, w), BF16),
             pltpu.VMEM((km, h), BF16),
             pltpu.VMEM((nblk, 2, kb, w), BF16),
-            pltpu.VMEM((km, w), BF16),
-            pltpu.VMEM((km, w), BF16),
+            pltpu.VMEM((npc, LT, w), BF16),
+            pltpu.VMEM((npc, LT, w), BF16),
             pltpu.VMEM((4, 8, h), F32),
             pltpu.VMEM((4, 2, 8, h), F32),
             pltpu.VMEM((4, h, LT), F32),
+            pltpu.VMEM((npc, nblk, kb, LT), F32),
             pltpu.VMEM((nblk, kb, km), F32),
-            pltpu.VMEM((nblk, kb, km), F32),
-            pltpu.VMEM((nblk, kb, km), F32),
-            pltpu.VMEM((slots, kb, km // 2), F32),
+            pltpu.VMEM((npc, nblk, kb, LT), F32),
+            pltpu.VMEM((slots, kb, LT), F32),
             pltpu.VMEM((ngx, kb, ab), F32),
-            pltpu.VMEM((ngx - 1, kb, ab), F32),
+            pltpu.VMEM((ngx, kb, ab), F32),
             dma((w // LT,)),
             dma((8,)),
             dma((4, 2)),
             dma((4, 2)),
             dma((4, 2)),
             dma((4, 2)),
-            dma((2,)),
+            dma((npc,)),
+            dma((npc,)),
             dma((slots,)),
             dma((slots,)),
-            dma((ngx - 1,)),
-            dma((ngx - 1,)),
+            dma((ngx,)),
+            dma((ngx,)),
         ],
         compiler_params=pltpu.CompilerParams(
             collective_id=0, has_side_effects=True, vmem_limit_bytes=VMEM_LIMIT

time: 46.7 us -> 40.9 us (0.88)
  Pallas kernels: 45.9 us -> 40.1 us
    pallas_call x1, Pallas kernels: 44.5 us -> 38.7 us  [shards(): pl.pallas_call(functools.partial(kernel, ngx, ngy), out_shape=(pltpu.VMEM...]
where the time goes in v3:
time: 40.9 us; the launch traced here: 40.7 us
  Pallas kernels  40.1 us (98%)
  between operations  0.64 us (2%)
    pallas_call x1, Pallas kernels, shards(): pl.pallas_call(functools.partial(kernel, ngx, ngy), out_shape=(pltpu.VMEM...  38.7 us
    pallas_call x1, Pallas kernels, shards(): pl.pallas_call(write_results, out_shape=(jax.ShapeDtypeStruct((2, h, w),...  1.37 us

profile of v3, /device:TPU:0, one launch (start us, length us, event | category | flops | bytes accessed | tf_op | source)
XLA Modules:
  0.0 40.7 jit_solution(14722762377864869531)
XLA Ops:
  0.6 38.7 %shard_map.104 = (f32[2,512,512]{2,1,0:T(8,128)S(1)}, f32[64,128]{1,0:T(8,128)S(1)}) custom-call(f32[2,512,512]{2,1,0:T(8,128)} %vel_h.1, f32[2,512,512]{2,1,0:T(8,128)} %obs_h.1, f32[512,512]{1,0:T(8,128)} %thick_h.1, f32[512,512]{1,0:T(8,128)} %rate_h.1, f32[512,512]{1,0:T(8,128)} %fric_h.1, s32[512,512]{1,0:T(8,128)} %mask_h.1, s32[512,512]{1,0:T(8,128)} %codes_h.1, ...), custom_call_target="tpu_custom_call" | custom-call | tf_op jit(solution)/shard_map/pallas_call | solution.py:392
  39.4 1.4 %shard_map.105 = (f32[2,512,512]{2,1,0:T(8,128)}, f32[64,128]{1,0:T(8,128)}) custom-call(f32[2,512,512]{2,1,0:T(8,128)S(1)} %get-tuple-element.6.adj, f32[64,128]{1,0:T(8,128)S(1)} %get-tuple-element.7.coef), custom_call_target="tpu_custom_call" | custom-call | tf_op jit(solution)/shard_map/pallas_call | solution.py:446

commit v4 on v3

--- a/solution.py
+++ b/solution.py
@@ -269,8 +269,8 @@
     take_edges(3)
     border(third)
 
-    nblk, kb, km = r_acc.shape
-    npc, ab = km // LT, km // ngx
+    npc, nblk, kb, _ = r_acc.shape
+    ab = npc * LT // ngx
     core = lax.rem(iy, 2)
     cell = iy // 2
     nbits = nblk.bit_length() - 1
@@ -296,22 +296,20 @@
             device_id=(ix, iy + 1 - 2 * core), device_id_type=MESH)
         pair.start()
         pairs.append(pair)
-    for p in range(npc):
-        r_acc[:, :, p * LT : (p + 1) * LT] = project(core, p)
 
     live = [[] for _ in range(npc)]
     flying = [[] for _ in range(npc)]
     slot = 0
     for stage in range(nbits + 1):
         for p in range(npc):
-            lanes = pl.ds(p * LT, LT)
             if stage == 0:
+                r_acc[p] = project(core, p)
                 pairs[p].wait_recv()
-                r_acc[:, :, lanes] += r_in[p]
+                r_acc[p] += r_in[p]
                 sent.append(pairs[p])
             for copy, dst, place in flying[p]:
                 copy.wait_recv()
-                r_acc[dst, :, lanes] += half_in[place]
+                r_acc[p, dst] += half_in[place]
                 sent.append(copy)
             flying[p] = []
             if stage < nbits:
@@ -323,7 +321,7 @@
                     src = fixed + (1 - bits[t]) * (1 << t)
                     dst = fixed + bits[t] * (1 << t)
                     copy = pltpu.make_async_remote_copy(
-                        r_acc.at[src, :, lanes], half_in.at[slot],
+                        r_acc.at[p, src], half_in.at[slot],
                         half_send.at[slot], half_recv.at[slot],
                         device_id=(ix, iy + (1 - 2 * bits[t]) * (2 << t)), device_id_type=MESH)
                     copy.start()
@@ -332,7 +330,7 @@
                 live[p].append(t)
             else:
                 for d in range(p * LT // ab, (p + 1) * LT // ab):
-                    z_out[d] = r_acc[cell, :, d * ab : (d + 1) * ab]
+                    z_out[d] = r_acc[p, cell, :, d * ab - p * LT : (d + 1) * ab - p * LT]
 
                     @pl.when(ix != d)
                     def _(d=d):
@@ -419,7 +417,7 @@
             pltpu.VMEM((4, 2, 8, h), F32),
             pltpu.VMEM((4, h, LT), F32),
             pltpu.VMEM((npc, nblk, kb, LT), F32),
-            pltpu.VMEM((nblk, kb, km), F32),
+            pltpu.VMEM((npc, nblk, kb, LT), F32),
             pltpu.VMEM((npc, nblk, kb, LT), F32),
             pltpu.VMEM((slots, kb, LT), F32),
             pltpu.VMEM((ngx, kb, ab), F32),

time: 40.9 us -> 40.8 us (level)
  no operation moved by 1% of the time
where the time goes in v4:
time: 40.8 us; the launch traced here: 40.7 us
  Pallas kernels  40.1 us (98%)
  between operations  0.64 us (2%)
    pallas_call x1, Pallas kernels, shards(): pl.pallas_call(functools.partial(kernel, ngx, ngy), out_shape=(pltpu.VMEM...  38.7 us
    pallas_call x1, Pallas kernels, shards(): pl.pallas_call(write_results, out_shape=(jax.ShapeDtypeStruct((2, h, w),...  1.37 us

profile of v4, /device:TPU:0, one launch (start us, length us, event | category | flops | bytes accessed | tf_op | source)
XLA Modules:
  0.0 40.7 jit_solution(16133094571167837987)
XLA Ops:
  0.6 38.7 %shard_map.104 = (f32[2,512,512]{2,1,0:T(8,128)S(1)}, f32[64,128]{1,0:T(8,128)S(1)}) custom-call(f32[2,512,512]{2,1,0:T(8,128)} %vel_h.1, f32[2,512,512]{2,1,0:T(8,128)} %obs_h.1, f32[512,512]{1,0:T(8,128)} %thick_h.1, f32[512,512]{1,0:T(8,128)} %rate_h.1, f32[512,512]{1,0:T(8,128)} %fric_h.1, s32[512,512]{1,0:T(8,128)} %mask_h.1, s32[512,512]{1,0:T(8,128)} %codes_h.1, ...), custom_call_target="tpu_custom_call" | custom-call | tf_op jit(solution)/shard_map/pallas_call | solution.py:390
  39.3 1.4 %shard_map.105 = (f32[2,512,512]{2,1,0:T(8,128)}, f32[64,128]{1,0:T(8,128)}) custom-call(f32[2,512,512]{2,1,0:T(8,128)S(1)} %get-tuple-element.6.adj, f32[64,128]{1,0:T(8,128)S(1)} %get-tuple-element.7.coef), custom_call_target="tpu_custom_call" | custom-call | tf_op jit(solution)/shard_map/pallas_call | solution.py:444
